TPU v7x, 128 devices: a whole 4x4x4 slice. The times are simulated.
128 devices in a mesh: patch: 32 (over x, z, core), grp: 4 (over y).
Axes of the slice: x: 4, y: 4, z: 4, core: 2. Of those that a mesh axis runs over, the one named last changes fastest.
Arguments:
- incident: float32 [16, 262144], P(None, ('patch', 'grp')), may hold values from -6 to 6
- self_term: float32 [262144], P(('patch', 'grp')), may hold values from 1 to 3
- near_field: bfloat16 [262144, 2304], P(('patch', 'grp')), may hold values from -0.125 to 0.125
- history: bfloat16 [8, 16, 262144], P(None, None, 'patch'), may hold values from -6 to 6
- ret_values: bfloat16 [32768, 128, 128], P(('patch', 'grp')), may hold values from -0.125 to 0.125
- slot_row: int32 [32768], P(('patch', 'grp')), may hold values from 0 to 15
- slot_col: int32 [32768], P(('patch', 'grp')), may hold values from 0 to 191
- slot_delay: int32 [32768], P(('patch', 'grp')), may hold values from 0 to 7
- live_count: int32 [128], P(('patch', 'grp')), may hold values from 32 to 256, as said below
Outputs:
- current: float32 [16, 262144], P(None, ('patch', 'grp'))
- newest: bfloat16 [16, 262144], P(None, 'patch')
Inputs may be any that keep to these rules, and one draw needn't show every extreme that they name: The first live_count[d] slots of shard d are live, the rest ignored; some shard has all 256 slots live.
All inputs are finite; a program needn't handle non-finite values.
Results may differ from a plain program's by a relative error of at most 0.0055.
Values may be sent and summed in bfloat16 or wider, within the bound.
No kernel may reach another device: no remote copies, remote signals or barrier semaphores. Data moves between devices by JAX's collectives and lax.ppermute only.
A program may use at most 128 MiB of HBM per device.

v0:
```python
import jax
import jax.numpy as jnp
from jax import lax
from jax.sharding import PartitionSpec as P

BLK = 128
DELAYS = 8
SWEEPS = 4
RB = 16
SLOTS = 256


def extended_2(block, sides, width):
    for axis, dim in sides:
        count = lax.axis_size(axis)
        forward = [(i, i + 1) for i in range(count - 1)]
        backward = [(target, source) for source, target in forward]
        low = lax.ppermute(
            lax.slice_in_dim(block, block.shape[dim] - width, None, axis=dim), axis, forward
        )
        high = lax.ppermute(lax.slice_in_dim(block, 0, width, axis=dim), axis, backward)
        block = jnp.concatenate([low, block, high], axis=dim)
    return block


def body(
    incident, self_term, near_field, history, ret_values, slot_row, slot_col, slot_delay, live_count
):
    waves = incident.shape[0]
    own_cols = incident.shape[1]
    group_idx = lax.axis_index("grp")
    window = extended_2(history, (("patch", 2),), history.shape[2])
    grouped = window.reshape(DELAYS, waves, window.shape[2] // BLK, BLK)
    limit = live_count[0]
    blocks = grouped[slot_delay, :, slot_col, :]
    prods = jnp.einsum("swj,sij->swi", blocks, ret_values, preferred_element_type=jnp.float32)
    alive = (jnp.arange(SLOTS, dtype=jnp.int32) < limit).astype(jnp.float32)
    onehot = (slot_row[None, :] == jnp.arange(RB, dtype=jnp.int32)[:, None]).astype(
        jnp.float32
    ) * alive[None, :]
    retarded = jnp.einsum("rs,swi->wri", onehot, prods, precision=lax.Precision.HIGHEST)
    rhs = incident - retarded.reshape(waves, own_cols)
    sweep_in = lax.dynamic_slice_in_dim(history[0], group_idx * own_cols, own_cols, 1)
    current = sweep_in.astype(jnp.float32)
    for sweep in range(SWEEPS):
        extended = extended_2(sweep_in, (("patch", 1),), BLK)
        coupling = lax.dot_general(
            extended, near_field, (((1,), (1,)), ((), ())), preferred_element_type=jnp.float32
        )
        current = (rhs - coupling) / self_term[None, :]
        sweep_in = current.astype(jnp.bfloat16)
    newest = lax.all_gather(sweep_in, "grp", axis=1, tiled=True)
    return (current, newest)


def solution(mesh):
    placed = (
        P(None, ("patch", "grp")),
        P(("patch", "grp")),
        P(("patch", "grp"), None),
        P(None, None, "patch"),
        P(("patch", "grp"), None, None),
        P(("patch", "grp")),
        P(("patch", "grp")),
        P(("patch", "grp")),
        P(("patch", "grp")),
    )
    return jax.shard_map(
        body,
        mesh=mesh,
        in_specs=placed,
        out_specs=(P(None, ("patch", "grp")), P(None, "patch")),
        check_vma=False,
    )
```

profile of v0, /device:TPU:6, one launch (start us, length us, event | category | flops | bytes accessed | tf_op | source)
XLA Modules:
  0.0 111.1 jit_solution(12761360910164445370)
XLA Ops:
  0.6 5.7 %collective-permute-start.1 = (bf16[8,16,8192]{2,1,0:T(8,128)(2,1)}, bf16[8,16,8192]{2,1,0:T(8,128)(2,1)S(1)}, u32[]{:S(2)}, u32[]{:S(2)}) collective-permute-start(bf16[8,16,8192]{2,1,0:T(8,128)(2,1)} %param.12), channel_id=1, source_target_pairs={{4,0},{8,4},{12,8},{16,12},{20,16},{24,20},{28,24},{32,28},{36,32}... | collective-permute-start | bytes 6291464 | tf_op jit(solution)/shard_map/ppermute | solution.py:21
  6.3 1.9 %collective-permute-start = (bf16[8,16,8192]{2,1,0:T(8,128)(2,1)}, bf16[8,16,8192]{2,1,0:T(8,128)(2,1)}, u32[]{:S(2)}, u32[]{:S(2)}) collective-permute-start(bf16[8,16,8192]{2,1,0:T(8,128)(2,1)} %param.12), channel_id=1, source_target_pairs={{0,4},{4,8},{8,12},{12,16},{16,20},{20,24},{24,28},{28,32},{32,36}... | collective-permute-start | bytes 6291464 | tf_op jit(solution)/shard_map/ppermute | solution.py:18
  8.2 1.0 slice.27
  9.2 5.8 %collective-permute-start.3 = (bf16[16,128]{1,0:T(8,128)(2,1)S(1)}, bf16[16,128]{1,0:T(8,128)(2,1)S(1)}, u32[]{:S(2)}, u32[]{:S(2)}) collective-permute-start(bf16[16,128]{1,0:T(8,128)(2,1)S(1)} %get-tuple-element.9), channel_id=1, source_target_pairs={{4,0},{8,4},{12,8},{16,12},{20,16},{24,20},{28,24},{32,28},{36,32}... | collective-permute-start | bytes 12296 | tf_op jit(solution)/shard_map/ppermute | solution.py:21
  15.0 1.9 %collective-permute-start.2 = (bf16[16,128]{1,0:T(8,128)(2,1)S(1)}, bf16[16,128]{1,0:T(8,128)(2,1)S(1)}, u32[]{:S(2)}, u32[]{:S(2)}) collective-permute-start(bf16[16,128]{1,0:T(8,128)(2,1)S(1)} %get-tuple-element.8), channel_id=1, source_target_pairs={{0,4},{4,8},{8,12},{12,16},{16,20},{20,24},{24,28},{28,32},{32,36}... | collective-permute-start | bytes 12296 | tf_op jit(solution)/shard_map/ppermute | solution.py:18
  17.6 0.7 fusion.36
  18.3 11.8 %collective-permute-done.1 = bf16[8,16,8192]{2,1,0:T(8,128)(2,1)S(1)} collective-permute-done((bf16[8,16,8192]{2,1,0:T(8,128)(2,1)}, bf16[8,16,8192]{2,1,0:T(8,128)(2,1)S(1)}, u32[]{:S(2)}, u32[]{:S(2)}) %collective-permute-start.1) | collective-permute-done | bytes 2097184 | tf_op jit(solution)/shard_map/ppermute | solution.py:21
  30.1 5.9 %collective-permute-done = bf16[8,16,8192]{2,1,0:T(8,128)(2,1)} collective-permute-done((bf16[8,16,8192]{2,1,0:T(8,128)(2,1)}, bf16[8,16,8192]{2,1,0:T(8,128)(2,1)}, u32[]{:S(2)}, u32[]{:S(2)}) %collective-permute-start) | collective-permute-done | bytes 2097184 | tf_op jit(solution)/shard_map/ppermute | solution.py:18
  36.1 7.2 %copy_bitcast_fusion = bf16[8,16,192,128]{3,1,2,0:T(8,128)(2,1)} fusion(bf16[8,16,8192]{2,1,0:T(8,128)(2,1)S(1)} %collective-permute-done.1, bf16[8,16,8192]{2,1,0:T(8,128)(2,1)} %param.12, bf16[8,16,8192]{2,1,0:T(8,128)(2,1)} %collective-permute-done), kind=kLoop, calls=%fused_computation.1 | loop fusion | flops 18874368 | bytes 12582912 | tf_op jit(solution)/shard_map/reshape | solution.py:33
  43.2 4.0 %gather_fusion = bf16[256,16,128]{2,1,0:T(8,128)(2,1)S(1)} fusion(bf16[8,16,192,128]{3,1,2,0:T(8,128)(2,1)} %copy_bitcast_fusion, s32[256]{0:T(256)S(1)} %fusion.36), kind=kCustom, calls=%fused_computation | custom fusion | bytes 2099200 | tf_op jit(solution)/shard_map/gather | solution.py:35
  47.2 0.0 copy-start.2
  47.3 0.0 slice-start
  47.3 6.9 %fusion.49 = f32[256,16,128]{2,1,0:T(8,128)S(1)} fusion(bf16[256,16,128]{2,1,0:T(8,128)(2,1)S(1)} %gather_fusion, bf16[256,128,128]{2,1,0:T(8,128)(2,1)} %param.13), kind=kOutput, calls=%fused_computation.62 | convolution fusion | flops 134217728 | bytes 11534336 | tf_op jit(solution)/shard_map/swj,sij->swi/dot_general | solution.py:36
  54.2 1.8 %fusion.7 = f32[16,128,16]{1,2,0:T(8,128)S(1)} fusion(f32[256,16,128]{2,1,0:T(8,128)S(1)} %fusion.49, f32[256]{0:T(256)S(1)} %compare_convert_fusion, s32[256]{0:T(256)S(1)} %copy-done.2), kind=kOutput, calls=%fused_computation.14 | convolution fusion | flops 100671488 | bytes 2230272 | tf_op jit(solution)/shard_map/rs,swi->wri/dot_general | solution.py:41
  56.0 0.0 copy-done.1
  56.0 0.1 bitcast_subtract_fusion
  56.0 0.0 slice-start.2
  56.1 6.3 %fusion.4 = bf16[16,2048]{1,0:T(8,128)(2,1)S(1)} fusion(f32[16,2048]{1,0:T(8,128)S(1)} %bitcast_subtract_fusion, bf16[2048,2304]{1,0:T(8,128)(2,1)} %param.11, bf16[16,128]{1,0:T(8,128)(2,1)S(1)} %collective-permute-done.3, bf16[16,2048]{1,0:T(8,128)(2,1)S(1)} %dynamic-slice_bitcast_fusion, bf16[16,128]{1,0:T(8,128)(2,1)S(1)} %collective-permute-done.2, ...), kind=kOutput, calls=%fused_computation.11 | convolution fusion | flops 151314432 | bytes 9715712 | tf_op jit(solution)/shard_map/dot_general | solution.py:47
  62.4 1.9 %collective-permute-start.5 = (bf16[16,128]{1,0:T(8,128)(2,1)S(1)}, bf16[16,128]{1,0:T(8,128)(2,1)S(1)}, u32[]{:S(2)}, u32[]{:S(2)}) collective-permute-start(bf16[16,128]{1,0:T(8,128)(2,1)S(1)} %get-tuple-element.7), channel_id=1, source_target_pairs={{4,0},{8,4},{12,8},{16,12},{20,16},{24,20},{28,24},{32,28},{36,32}... | collective-permute-start | bytes 12296 | tf_op jit(solution)/shard_map/ppermute | solution.py:21
  64.3 2.4 %collective-permute-start.4 = (bf16[16,128]{1,0:T(8,128)(2,1)S(1)}, bf16[16,128]{1,0:T(8,128)(2,1)S(1)}, u32[]{:S(2)}, u32[]{:S(2)}) collective-permute-start(bf16[16,128]{1,0:T(8,128)(2,1)S(1)} %get-tuple-element.6), channel_id=1, source_target_pairs={{0,4},{4,8},{8,12},{12,16},{16,20},{20,24},{24,28},{28,32},{32,36}... | collective-permute-start | bytes 12296 | tf_op jit(solution)/shard_map/ppermute | solution.py:18
  66.8 4.6 %collective-permute-done.4 = bf16[16,128]{1,0:T(8,128)(2,1)S(1)} collective-permute-done((bf16[16,128]{1,0:T(8,128)(2,1)S(1)}, bf16[16,128]{1,0:T(8,128)(2,1)S(1)}, u32[]{:S(2)}, u32[]{:S(2)}) %collective-permute-start.4) | collective-permute-done | bytes 4128 | tf_op jit(solution)/shard_map/ppermute | solution.py:18
  71.4 2.5 %fusion.5 = bf16[16,2048]{1,0:T(8,128)(2,1)S(1)} fusion(f32[16,2048]{1,0:T(8,128)S(1)} %bitcast_subtract_fusion, bf16[2048,2304]{1,0:T(8,128)(2,1)S(1)} %bitcast.23, bf16[16,128]{1,0:T(8,128)(2,1)S(1)} %collective-permute-done.5, bf16[16,2048]{1,0:T(8,128)(2,1)S(1)} %fusion.4, bf16[16,128]{1,0:T(8,128)(2,1)S(1)} %collective-permute-done.4, f32[2048]{0:T(1024)S(1)} %copy-done), kind=kOutput, calls=%fused_computation.12 | convolution fusion | flops 151314432 | bytes 9715712 | tf_op jit(solution)/shard_map/dot_general | solution.py:47
  73.9 1.9 %collective-permute-start.7 = (bf16[16,128]{1,0:T(8,128)(2,1)S(1)}, bf16[16,128]{1,0:T(8,128)(2,1)S(1)}, u32[]{:S(2)}, u32[]{:S(2)}) collective-permute-start(bf16[16,128]{1,0:T(8,128)(2,1)S(1)} %get-tuple-element.5), channel_id=1, source_target_pairs={{4,0},{8,4},{12,8},{16,12},{20,16},{24,20},{28,24},{32,28},{36,32}... | collective-permute-start | bytes 12296 | tf_op jit(solution)/shard_map/ppermute | solution.py:21
  75.9 2.4 %collective-permute-start.6 = (bf16[16,128]{1,0:T(8,128)(2,1)S(1)}, bf16[16,128]{1,0:T(8,128)(2,1)S(1)}, u32[]{:S(2)}, u32[]{:S(2)}) collective-permute-start(bf16[16,128]{1,0:T(8,128)(2,1)S(1)} %get-tuple-element.4), channel_id=1, source_target_pairs={{0,4},{4,8},{8,12},{12,16},{16,20},{20,24},{24,28},{28,32},{32,36}... | collective-permute-start | bytes 12296 | tf_op jit(solution)/shard_map/ppermute | solution.py:18
  78.3 4.6 %collective-permute-done.6 = bf16[16,128]{1,0:T(8,128)(2,1)S(1)} collective-permute-done((bf16[16,128]{1,0:T(8,128)(2,1)S(1)}, bf16[16,128]{1,0:T(8,128)(2,1)S(1)}, u32[]{:S(2)}, u32[]{:S(2)}) %collective-permute-start.6) | collective-permute-done | bytes 4128 | tf_op jit(solution)/shard_map/ppermute | solution.py:18
  82.9 2.5 %fusion.6 = bf16[16,2048]{1,0:T(8,128)(2,1)S(1)} fusion(f32[16,2048]{1,0:T(8,128)S(1)} %bitcast_subtract_fusion, bf16[2048,2304]{1,0:T(8,128)(2,1)S(1)} %bitcast.23, bf16[16,128]{1,0:T(8,128)(2,1)S(1)} %collective-permute-done.7, bf16[16,2048]{1,0:T(8,128)(2,1)S(1)} %fusion.5, bf16[16,128]{1,0:T(8,128)(2,1)S(1)} %collective-permute-done.6, f32[2048]{0:T(1024)S(1)} %copy-done), kind=kOutput, calls=%fused_computation.13 | convolution fusion | flops 151314432 | bytes 9715712 | tf_op jit(solution)/shard_map/dot_general | solution.py:47
  85.5 1.9 %collective-permute-start.9 = (bf16[16,128]{1,0:T(8,128)(2,1)S(1)}, bf16[16,128]{1,0:T(8,128)(2,1)S(1)}, u32[]{:S(2)}, u32[]{:S(2)}) collective-permute-start(bf16[16,128]{1,0:T(8,128)(2,1)S(1)} %get-tuple-element.3), channel_id=1, source_target_pairs={{4,0},{8,4},{12,8},{16,12},{20,16},{24,20},{28,24},{32,28},{36,32}... | collective-permute-start | bytes 12296 | tf_op jit(solution)/shard_map/ppermute | solution.py:21
  87.4 2.4 %collective-permute-start.8 = (bf16[16,128]{1,0:T(8,128)(2,1)S(1)}, bf16[16,128]{1,0:T(8,128)(2,1)S(1)}, u32[]{:S(2)}, u32[]{:S(2)}) collective-permute-start(bf16[16,128]{1,0:T(8,128)(2,1)S(1)} %get-tuple-element.2), channel_id=1, source_target_pairs={{0,4},{4,8},{8,12},{12,16},{16,20},{20,24},{24,28},{28,32},{32,36}... | collective-permute-start | bytes 12296 | tf_op jit(solution)/shard_map/ppermute | solution.py:18
  89.8 4.6 %collective-permute-done.8 = bf16[16,128]{1,0:T(8,128)(2,1)S(1)} collective-permute-done((bf16[16,128]{1,0:T(8,128)(2,1)S(1)}, bf16[16,128]{1,0:T(8,128)(2,1)S(1)}, u32[]{:S(2)}, u32[]{:S(2)}) %collective-permute-start.8) | collective-permute-done | bytes 4128 | tf_op jit(solution)/shard_map/ppermute | solution.py:18
  94.4 3.2 %fusion.48 = (bf16[16,2048]{1,0:T(8,128)(2,1)S(1)}, f32[16,2048]{1,0:T(8,128)}) fusion(f32[2048]{0:T(1024)S(1)} %copy-done, f32[16,2048]{1,0:T(8,128)S(1)} %bitcast_subtract_fusion, bf16[2048,2304]{1,0:T(8,128)(2,1)S(1)} %bitcast.23, bf16[16,128]{1,0:T(8,128)(2,1)S(1)} %collective-permute-done.9, bf16[16,2048]{1,0:T(8,128)(2,1)S(1)} %fusion.6, ...), kind=kOutput, calls=%fused_computation.61 | convolution fusion | flops 151314432 | bytes 9846784 | tf_op jit(solution)/shard_map/dot_general | solution.py:47
  97.6 12.8 %all_gather.3 = bf16[16,8192]{1,0:T(8,128)(2,1)S(1)} all-gather(bf16[16,2048]{1,0:T(8,128)(2,1)S(1)} %get-tuple-element.10), channel_id=1, replica_groups=mesh['patch'=32,'grp'=4] {'grp'}, dimensions={1}, use_global_device_ids=true | all-gather | bytes 327680 | tf_op jit(solution)/shard_map/all_gather | solution.py:52
  110.4 0.7 copy.21
  (20 shorter events, 0.1 us)
Async XLA Ops:
  0.6 29.5 %collective-permute-start.1 = (bf16[8,16,8192]{2,1,0:T(8,128)(2,1)}, bf16[8,16,8192]{2,1,0:T(8,128)(2,1)S(1)}, u32[]{:S(2)}, u32[]{:S(2)}) collective-permute-start(bf16[8,16,8192]{2,1,0:T(8,128)(2,1)} %param.12), channel_id=1, source_target_pairs={{4,0},{8,4},{12,8},{16,12},{20,16},{24,20},{28,24},{32,28},{36,32}... | collective-permute-start | bytes 6291464 | tf_op jit(solution)/shard_map/ppermute | solution.py:21
  6.3 29.8 %collective-permute-start = (bf16[8,16,8192]{2,1,0:T(8,128)(2,1)}, bf16[8,16,8192]{2,1,0:T(8,128)(2,1)}, u32[]{:S(2)}, u32[]{:S(2)}) collective-permute-start(bf16[8,16,8192]{2,1,0:T(8,128)(2,1)} %param.12), channel_id=1, source_target_pairs={{0,4},{4,8},{8,12},{12,16},{16,20},{20,24},{24,28},{28,32},{32,36}... | collective-permute-start | bytes 6291464 | tf_op jit(solution)/shard_map/ppermute | solution.py:18
  9.2 46.8 %collective-permute-start.3 = (bf16[16,128]{1,0:T(8,128)(2,1)S(1)}, bf16[16,128]{1,0:T(8,128)(2,1)S(1)}, u32[]{:S(2)}, u32[]{:S(2)}) collective-permute-start(bf16[16,128]{1,0:T(8,128)(2,1)S(1)} %get-tuple-element.9), channel_id=1, source_target_pairs={{4,0},{8,4},{12,8},{16,12},{20,16},{24,20},{28,24},{32,28},{36,32}... | collective-permute-start | bytes 12296 | tf_op jit(solution)/shard_map/ppermute | solution.py:21
  15.0 41.1 %collective-permute-start.2 = (bf16[16,128]{1,0:T(8,128)(2,1)S(1)}, bf16[16,128]{1,0:T(8,128)(2,1)S(1)}, u32[]{:S(2)}, u32[]{:S(2)}) collective-permute-start(bf16[16,128]{1,0:T(8,128)(2,1)S(1)} %get-tuple-element.8), channel_id=1, source_target_pairs={{0,4},{4,8},{8,12},{12,16},{16,20},{20,24},{24,28},{28,32},{32,36}... | collective-permute-start | bytes 12296 | tf_op jit(solution)/shard_map/ppermute | solution.py:18
  47.2 7.0 %copy-start.2 = (s32[256]{0:T(256)S(1)}, s32[256]{0:T(256)}, u32[]{:S(2)}) copy-start(s32[256]{0:T(256)} %param.14) | copy-start | bytes 3076
  47.3 8.7 %copy-start.1 = (f32[16,2048]{1,0:T(8,128)S(1)}, f32[16,2048]{1,0:T(8,128)}, u32[]{:S(2)}) copy-start(f32[16,2048]{1,0:T(8,128)} %param.9) | copy-start | bytes 393220
  47.3 8.8 %copy-start = (f32[2048]{0:T(1024)S(1)}, f32[2048]{0:T(1024)}, u32[]{:S(2)}) copy-start(f32[2048]{0:T(1024)} %param.10) | copy-start | bytes 24580
  47.3 24.1 %slice-start = ((s8[9437184]{0:T(1024)(128)(4,1)}), s8[4194304]{0:T(1024)(128)(4,1)S(1)}, s32[]{:S(2)}) async-start(s8[9437184]{0:T(1024)(128)(4,1)} %bitcast.22), calls=%async_computation | async-start | bytes 8388608
  47.3 24.1 %slice-start.1 = ((s8[9437184]{0:T(1024)(128)(4,1)}), s8[4194304]{0:T(1024)(128)(4,1)S(1)}, s32[]{:S(2)}) async-start(s8[9437184]{0:T(1024)(128)(4,1)} %bitcast.22), calls=%async_computation.1 | async-start | bytes 8388608
  56.0 15.3 %slice-start.2 = ((s8[9437184]{0:T(1024)(128)(4,1)}), s8[1048576]{0:T(1024)(128)(4,1)S(1)}, s32[]{:S(2)}) async-start(s8[9437184]{0:T(1024)(128)(4,1)} %bitcast.22), calls=%async_computation.2 | async-start | bytes 2097152
  62.4 4.3 %collective-permute-start.5 = (bf16[16,128]{1,0:T(8,128)(2,1)S(1)}, bf16[16,128]{1,0:T(8,128)(2,1)S(1)}, u32[]{:S(2)}, u32[]{:S(2)}) collective-permute-start(bf16[16,128]{1,0:T(8,128)(2,1)S(1)} %get-tuple-element.7), channel_id=1, source_target_pairs={{4,0},{8,4},{12,8},{16,12},{20,16},{24,20},{28,24},{32,28},{36,32}... | collective-permute-start | bytes 12296 | tf_op jit(solution)/shard_map/ppermute | solution.py:21
  64.3 7.0 %collective-permute-start.4 = (bf16[16,128]{1,0:T(8,128)(2,1)S(1)}, bf16[16,128]{1,0:T(8,128)(2,1)S(1)}, u32[]{:S(2)}, u32[]{:S(2)}) collective-permute-start(bf16[16,128]{1,0:T(8,128)(2,1)S(1)} %get-tuple-element.6), channel_id=1, source_target_pairs={{0,4},{4,8},{8,12},{12,16},{16,20},{20,24},{24,28},{28,32},{32,36}... | collective-permute-start | bytes 12296 | tf_op jit(solution)/shard_map/ppermute | solution.py:18
  73.9 4.3 %collective-permute-start.7 = (bf16[16,128]{1,0:T(8,128)(2,1)S(1)}, bf16[16,128]{1,0:T(8,128)(2,1)S(1)}, u32[]{:S(2)}, u32[]{:S(2)}) collective-permute-start(bf16[16,128]{1,0:T(8,128)(2,1)S(1)} %get-tuple-element.5), channel_id=1, source_target_pairs={{4,0},{8,4},{12,8},{16,12},{20,16},{24,20},{28,24},{32,28},{36,32}... | collective-permute-start | bytes 12296 | tf_op jit(solution)/shard_map/ppermute | solution.py:21
  75.9 7.0 %collective-permute-start.6 = (bf16[16,128]{1,0:T(8,128)(2,1)S(1)}, bf16[16,128]{1,0:T(8,128)(2,1)S(1)}, u32[]{:S(2)}, u32[]{:S(2)}) collective-permute-start(bf16[16,128]{1,0:T(8,128)(2,1)S(1)} %get-tuple-element.4), channel_id=1, source_target_pairs={{0,4},{4,8},{8,12},{12,16},{16,20},{20,24},{24,28},{28,32},{32,36}... | collective-permute-start | bytes 12296 | tf_op jit(solution)/shard_map/ppermute | solution.py:18
  85.5 4.3 %collective-permute-start.9 = (bf16[16,128]{1,0:T(8,128)(2,1)S(1)}, bf16[16,128]{1,0:T(8,128)(2,1)S(1)}, u32[]{:S(2)}, u32[]{:S(2)}) collective-permute-start(bf16[16,128]{1,0:T(8,128)(2,1)S(1)} %get-tuple-element.3), channel_id=1, source_target_pairs={{4,0},{8,4},{12,8},{16,12},{20,16},{24,20},{28,24},{32,28},{36,32}... | collective-permute-start | bytes 12296 | tf_op jit(solution)/shard_map/ppermute | solution.py:21
  87.4 7.0 %collective-permute-start.8 = (bf16[16,128]{1,0:T(8,128)(2,1)S(1)}, bf16[16,128]{1,0:T(8,128)(2,1)S(1)}, u32[]{:S(2)}, u32[]{:S(2)}) collective-permute-start(bf16[16,128]{1,0:T(8,128)(2,1)S(1)} %get-tuple-element.2), channel_id=1, source_target_pairs={{0,4},{4,8},{8,12},{12,16},{16,20},{20,24},{24,28},{28,32},{32,36}... | collective-permute-start | bytes 12296 | tf_op jit(solution)/shard_map/ppermute | solution.py:18
where the time goes:
time: 112 us; the launch traced here: 111 us
  waiting for transfers between devices  31.6 us (28%)
  starting transfers between devices  28.2 us (25%)
  matrix products  23.2 us (21%)
  blocking collectives  12.8 us (11%)
  other arithmetic  7.93 us (7%)
  local copies, waits for them, and re-layouts  5.77 us (5%)
  between operations  1.54 us (1%)
    ppermute x5, waiting for transfers between devices, extended_2(): lax.ppermute(lax.slice_in_dim(block, block.shape[dim] - width, None, axis...  19.8 us
    ppermute x5, starting transfers between devices, extended_2(): lax.ppermute(lax.slice_in_dim(block, 0, width, axis=dim), axis, backward)  17.2 us
    dot_general x4, matrix products, body(): lax.dot_general(extended, near_field, (((1,), (1,)), ((), ())), preferred...  14.6 us
    all_gather x1, blocking collectives, body(): newest = lax.all_gather(sweep_in, 'grp', axis=1, tiled=True)  12.8 us
    ppermute x5, waiting for transfers between devices, extended_2(): lax.ppermute(lax.slice_in_dim(block, 0, width, axis=dim), axis, backward)  11.9 us
    ppermute x5, starting transfers between devices, extended_2(): lax.ppermute(lax.slice_in_dim(block, block.shape[dim] - width, None, axis...  11.1 us
    reshape x1, other arithmetic, body(): grouped = window.reshape(DELAYS, waves, window.shape[2] // BLK, BLK)  7.16 us
    dot_general x1, matrix products, body(): jnp.einsum('swj,sij->swi', blocks, ret_values, preferred_element_type=jnp...  6.91 us
  transfers between devices with their start and end apart: 10, of which 5 were waited for; matrix products, arithmetic and copies ran while one was open for 19% of the time, Pallas kernels for 0%

commit v1 on v0

--- a/solution.py
+++ b/solution.py
@@ -49,7 +49,9 @@
         )
         current = (rhs - coupling) / self_term[None, :]
         sweep_in = current.astype(jnp.bfloat16)
-    newest = lax.all_gather(sweep_in, "grp", axis=1, tiled=True)
+    newest = jnp.concatenate(
+        lax.all_to_all(jnp.stack([sweep_in] * lax.axis_size("grp")), "grp", 0, 0), axis=1
+    )
     return (current, newest)
 
 

time: 112 us -> 110 us (0.982)
  blocking collectives: 12.8 us -> 10.9 us
    all_gather x1 -> x0, blocking collectives: 12.8 us -> none  [body(): newest = lax.all_gather(sweep_in, 'grp', axis=1, tiled=True)]
    all_to_all x0 -> x1, blocking collectives: none -> 10.9 us  [body(): lax.all_to_all(jnp.stack([sweep_in] * lax.axis_size('grp')), 'grp', 0, 0)]
  transfers between devices with their start and end apart: 10 -> 10, of which waited for: 5 -> 5; matrix products, arithmetic and copies ran while one was open for 19% -> 20% of each run, Pallas kernels for 0% -> 0%
where the time goes in v1:
time: 110 us; the launch traced here: 109 us
  waiting for transfers between devices  31.6 us (29%)
  starting transfers between devices  28.2 us (26%)
  matrix products  23.2 us (21%)
  blocking collectives  10.9 us (10%)
  other arithmetic  7.93 us (7%)
  local copies, waits for them, and re-layouts  5.81 us (5%)
  between operations  1.54 us (1%)
    ppermute x5, waiting for transfers between devices, extended_2(): lax.ppermute(lax.slice_in_dim(block, block.shape[dim] - width, None, axis...  19.8 us
    ppermute x5, starting transfers between devices, extended_2(): lax.ppermute(lax.slice_in_dim(block, 0, width, axis=dim), axis, backward)  17.2 us
    dot_general x4, matrix products, body(): lax.dot_general(extended, near_field, (((1,), (1,)), ((), ())), preferred...  14.6 us
    ppermute x5, waiting for transfers between devices, extended_2(): lax.ppermute(lax.slice_in_dim(block, 0, width, axis=dim), axis, backward)  11.9 us
    ppermute x5, starting transfers between devices, extended_2(): lax.ppermute(lax.slice_in_dim(block, block.shape[dim] - width, None, axis...  11.1 us
    all_to_all x1, blocking collectives, body(): lax.all_to_all(jnp.stack([sweep_in] * lax.axis_size('grp')), 'grp', 0, 0)  10.9 us
    reshape x1, other arithmetic, body(): grouped = window.reshape(DELAYS, waves, window.shape[2] // BLK, BLK)  7.16 us
    dot_general x1, matrix products, body(): jnp.einsum('swj,sij->swi', blocks, ret_values, preferred_element_type=jnp...  6.91 us
  transfers between devices with their start and end apart: 10, of which 5 were waited for; matrix products, arithmetic and copies ran while one was open for 20% of the time, Pallas kernels for 0%

profile of v1, /device:TPU:6, one launch (start us, length us, event | category | flops | bytes accessed | tf_op | source)
XLA Modules:
  0.0 109.3 jit_solution(15193734571890088657)
XLA Ops:
  0.6 5.7 %collective-permute-start.1 = (bf16[8,16,8192]{2,1,0:T(8,128)(2,1)}, bf16[8,16,8192]{2,1,0:T(8,128)(2,1)S(1)}, u32[]{:S(2)}, u32[]{:S(2)}) collective-permute-start(bf16[8,16,8192]{2,1,0:T(8,128)(2,1)} %param.12), channel_id=1, source_target_pairs={{4,0},{8,4},{12,8},{16,12},{20,16},{24,20},{28,24},{32,28},{36,32}... | collective-permute-start | bytes 6291464 | tf_op jit(solution)/shard_map/ppermute | solution.py:21
  6.3 1.9 %collective-permute-start = (bf16[8,16,8192]{2,1,0:T(8,128)(2,1)}, bf16[8,16,8192]{2,1,0:T(8,128)(2,1)}, u32[]{:S(2)}, u32[]{:S(2)}) collective-permute-start(bf16[8,16,8192]{2,1,0:T(8,128)(2,1)} %param.12), channel_id=1, source_target_pairs={{0,4},{4,8},{8,12},{12,16},{16,20},{20,24},{24,28},{28,32},{32,36}... | collective-permute-start | bytes 6291464 | tf_op jit(solution)/shard_map/ppermute | solution.py:18
  8.2 1.0 slice.27
  9.2 5.8 %collective-permute-start.3 = (bf16[16,128]{1,0:T(8,128)(2,1)S(1)}, bf16[16,128]{1,0:T(8,128)(2,1)S(1)}, u32[]{:S(2)}, u32[]{:S(2)}) collective-permute-start(bf16[16,128]{1,0:T(8,128)(2,1)S(1)} %get-tuple-element.9), channel_id=1, source_target_pairs={{4,0},{8,4},{12,8},{16,12},{20,16},{24,20},{28,24},{32,28},{36,32}... | collective-permute-start | bytes 12296 | tf_op jit(solution)/shard_map/ppermute | solution.py:21
  15.0 1.9 %collective-permute-start.2 = (bf16[16,128]{1,0:T(8,128)(2,1)S(1)}, bf16[16,128]{1,0:T(8,128)(2,1)S(1)}, u32[]{:S(2)}, u32[]{:S(2)}) collective-permute-start(bf16[16,128]{1,0:T(8,128)(2,1)S(1)} %get-tuple-element.8), channel_id=1, source_target_pairs={{0,4},{4,8},{8,12},{12,16},{16,20},{20,24},{24,28},{28,32},{32,36}... | collective-permute-start | bytes 12296 | tf_op jit(solution)/shard_map/ppermute | solution.py:18
  17.6 0.7 fusion.36
  18.3 11.8 %collective-permute-done.1 = bf16[8,16,8192]{2,1,0:T(8,128)(2,1)S(1)} collective-permute-done((bf16[8,16,8192]{2,1,0:T(8,128)(2,1)}, bf16[8,16,8192]{2,1,0:T(8,128)(2,1)S(1)}, u32[]{:S(2)}, u32[]{:S(2)}) %collective-permute-start.1) | collective-permute-done | bytes 2097184 | tf_op jit(solution)/shard_map/ppermute | solution.py:21
  30.1 5.9 %collective-permute-done = bf16[8,16,8192]{2,1,0:T(8,128)(2,1)} collective-permute-done((bf16[8,16,8192]{2,1,0:T(8,128)(2,1)}, bf16[8,16,8192]{2,1,0:T(8,128)(2,1)}, u32[]{:S(2)}, u32[]{:S(2)}) %collective-permute-start) | collective-permute-done | bytes 2097184 | tf_op jit(solution)/shard_map/ppermute | solution.py:18
  36.1 7.2 %copy_bitcast_fusion = bf16[8,16,192,128]{3,1,2,0:T(8,128)(2,1)} fusion(bf16[8,16,8192]{2,1,0:T(8,128)(2,1)S(1)} %collective-permute-done.1, bf16[8,16,8192]{2,1,0:T(8,128)(2,1)} %param.12, bf16[8,16,8192]{2,1,0:T(8,128)(2,1)} %collective-permute-done), kind=kLoop, calls=%fused_computation.1 | loop fusion | flops 18874368 | bytes 12582912 | tf_op jit(solution)/shard_map/reshape | solution.py:33
  43.2 4.0 %gather_fusion = bf16[256,16,128]{2,1,0:T(8,128)(2,1)S(1)} fusion(bf16[8,16,192,128]{3,1,2,0:T(8,128)(2,1)} %copy_bitcast_fusion, s32[256]{0:T(256)S(1)} %fusion.36), kind=kCustom, calls=%fused_computation | custom fusion | bytes 2099200 | tf_op jit(solution)/shard_map/gather | solution.py:35
  47.2 0.0 copy-start.2
  47.3 0.0 slice-start
  47.3 6.9 %fusion.49 = f32[256,16,128]{2,1,0:T(8,128)S(1)} fusion(bf16[256,16,128]{2,1,0:T(8,128)(2,1)S(1)} %gather_fusion, bf16[256,128,128]{2,1,0:T(8,128)(2,1)} %param.13), kind=kOutput, calls=%fused_computation.62 | convolution fusion | flops 134217728 | bytes 11534336 | tf_op jit(solution)/shard_map/swj,sij->swi/dot_general | solution.py:36
  54.2 1.8 %fusion.7 = f32[16,128,16]{1,2,0:T(8,128)S(1)} fusion(f32[256,16,128]{2,1,0:T(8,128)S(1)} %fusion.49, f32[256]{0:T(256)S(1)} %compare_convert_fusion, s32[256]{0:T(256)S(1)} %copy-done.2), kind=kOutput, calls=%fused_computation.14 | convolution fusion | flops 100671488 | bytes 2230272 | tf_op jit(solution)/shard_map/rs,swi->wri/dot_general | solution.py:41
  56.0 0.0 copy-done.1
  56.0 0.1 bitcast_subtract_fusion
  56.0 0.0 slice-start.2
  56.1 6.3 %fusion.4 = bf16[16,2048]{1,0:T(8,128)(2,1)S(1)} fusion(f32[16,2048]{1,0:T(8,128)S(1)} %bitcast_subtract_fusion, bf16[2048,2304]{1,0:T(8,128)(2,1)} %param.11, bf16[16,128]{1,0:T(8,128)(2,1)S(1)} %collective-permute-done.3, bf16[16,2048]{1,0:T(8,128)(2,1)S(1)} %dynamic-slice_bitcast_fusion, bf16[16,128]{1,0:T(8,128)(2,1)S(1)} %collective-permute-done.2, ...), kind=kOutput, calls=%fused_computation.11 | convolution fusion | flops 151314432 | bytes 9715712 | tf_op jit(solution)/shard_map/dot_general | solution.py:47
  62.4 1.9 %collective-permute-start.5 = (bf16[16,128]{1,0:T(8,128)(2,1)S(1)}, bf16[16,128]{1,0:T(8,128)(2,1)S(1)}, u32[]{:S(2)}, u32[]{:S(2)}) collective-permute-start(bf16[16,128]{1,0:T(8,128)(2,1)S(1)} %get-tuple-element.7), channel_id=1, source_target_pairs={{4,0},{8,4},{12,8},{16,12},{20,16},{24,20},{28,24},{32,28},{36,32}... | collective-permute-start | bytes 12296 | tf_op jit(solution)/shard_map/ppermute | solution.py:21
  64.3 2.4 %collective-permute-start.4 = (bf16[16,128]{1,0:T(8,128)(2,1)S(1)}, bf16[16,128]{1,0:T(8,128)(2,1)S(1)}, u32[]{:S(2)}, u32[]{:S(2)}) collective-permute-start(bf16[16,128]{1,0:T(8,128)(2,1)S(1)} %get-tuple-element.6), channel_id=1, source_target_pairs={{0,4},{4,8},{8,12},{12,16},{16,20},{20,24},{24,28},{28,32},{32,36}... | collective-permute-start | bytes 12296 | tf_op jit(solution)/shard_map/ppermute | solution.py:18
  66.8 4.6 %collective-permute-done.4 = bf16[16,128]{1,0:T(8,128)(2,1)S(1)} collective-permute-done((bf16[16,128]{1,0:T(8,128)(2,1)S(1)}, bf16[16,128]{1,0:T(8,128)(2,1)S(1)}, u32[]{:S(2)}, u32[]{:S(2)}) %collective-permute-start.4) | collective-permute-done | bytes 4128 | tf_op jit(solution)/shard_map/ppermute | solution.py:18
  71.4 2.5 %fusion.5 = bf16[16,2048]{1,0:T(8,128)(2,1)S(1)} fusion(f32[16,2048]{1,0:T(8,128)S(1)} %bitcast_subtract_fusion, bf16[2048,2304]{1,0:T(8,128)(2,1)S(1)} %bitcast.26, bf16[16,128]{1,0:T(8,128)(2,1)S(1)} %collective-permute-done.5, bf16[16,2048]{1,0:T(8,128)(2,1)S(1)} %fusion.4, bf16[16,128]{1,0:T(8,128)(2,1)S(1)} %collective-permute-done.4, f32[2048]{0:T(1024)S(1)} %copy-done), kind=kOutput, calls=%fused_computation.12 | convolution fusion | flops 151314432 | bytes 9715712 | tf_op jit(solution)/shard_map/dot_general | solution.py:47
  73.9 1.9 %collective-permute-start.7 = (bf16[16,128]{1,0:T(8,128)(2,1)S(1)}, bf16[16,128]{1,0:T(8,128)(2,1)S(1)}, u32[]{:S(2)}, u32[]{:S(2)}) collective-permute-start(bf16[16,128]{1,0:T(8,128)(2,1)S(1)} %get-tuple-element.5), channel_id=1, source_target_pairs={{4,0},{8,4},{12,8},{16,12},{20,16},{24,20},{28,24},{32,28},{36,32}... | collective-permute-start | bytes 12296 | tf_op jit(solution)/shard_map/ppermute | solution.py:21
  75.9 2.4 %collective-permute-start.6 = (bf16[16,128]{1,0:T(8,128)(2,1)S(1)}, bf16[16,128]{1,0:T(8,128)(2,1)S(1)}, u32[]{:S(2)}, u32[]{:S(2)}) collective-permute-start(bf16[16,128]{1,0:T(8,128)(2,1)S(1)} %get-tuple-element.4), channel_id=1, source_target_pairs={{0,4},{4,8},{8,12},{12,16},{16,20},{20,24},{24,28},{28,32},{32,36}... | collective-permute-start | bytes 12296 | tf_op jit(solution)/shard_map/ppermute | solution.py:18
  78.3 4.6 %collective-permute-done.6 = bf16[16,128]{1,0:T(8,128)(2,1)S(1)} collective-permute-done((bf16[16,128]{1,0:T(8,128)(2,1)S(1)}, bf16[16,128]{1,0:T(8,128)(2,1)S(1)}, u32[]{:S(2)}, u32[]{:S(2)}) %collective-permute-start.6) | collective-permute-done | bytes 4128 | tf_op jit(solution)/shard_map/ppermute | solution.py:18
  82.9 2.5 %fusion.6 = bf16[16,2048]{1,0:T(8,128)(2,1)S(1)} fusion(f32[16,2048]{1,0:T(8,128)S(1)} %bitcast_subtract_fusion, bf16[2048,2304]{1,0:T(8,128)(2,1)S(1)} %bitcast.26, bf16[16,128]{1,0:T(8,128)(2,1)S(1)} %collective-permute-done.7, bf16[16,2048]{1,0:T(8,128)(2,1)S(1)} %fusion.5, bf16[16,128]{1,0:T(8,128)(2,1)S(1)} %collective-permute-done.6, f32[2048]{0:T(1024)S(1)} %copy-done), kind=kOutput, calls=%fused_computation.13 | convolution fusion | flops 151314432 | bytes 9715712 | tf_op jit(solution)/shard_map/dot_general | solution.py:47
  85.5 1.9 %collective-permute-start.9 = (bf16[16,128]{1,0:T(8,128)(2,1)S(1)}, bf16[16,128]{1,0:T(8,128)(2,1)S(1)}, u32[]{:S(2)}, u32[]{:S(2)}) collective-permute-start(bf16[16,128]{1,0:T(8,128)(2,1)S(1)} %get-tuple-element.3), channel_id=1, source_target_pairs={{4,0},{8,4},{12,8},{16,12},{20,16},{24,20},{28,24},{32,28},{36,32}... | collective-permute-start | bytes 12296 | tf_op jit(solution)/shard_map/ppermute | solution.py:21
  87.4 2.4 %collective-permute-start.8 = (bf16[16,128]{1,0:T(8,128)(2,1)S(1)}, bf16[16,128]{1,0:T(8,128)(2,1)S(1)}, u32[]{:S(2)}, u32[]{:S(2)}) collective-permute-start(bf16[16,128]{1,0:T(8,128)(2,1)S(1)} %get-tuple-element.2), channel_id=1, source_target_pairs={{0,4},{4,8},{8,12},{12,16},{16,20},{20,24},{24,28},{28,32},{32,36}... | collective-permute-start | bytes 12296 | tf_op jit(solution)/shard_map/ppermute | solution.py:18
  89.8 4.6 %collective-permute-done.8 = bf16[16,128]{1,0:T(8,128)(2,1)S(1)} collective-permute-done((bf16[16,128]{1,0:T(8,128)(2,1)S(1)}, bf16[16,128]{1,0:T(8,128)(2,1)S(1)}, u32[]{:S(2)}, u32[]{:S(2)}) %collective-permute-start.8) | collective-permute-done | bytes 4128 | tf_op jit(solution)/shard_map/ppermute | solution.py:18
  94.4 3.2 %fusion.48 = (bf16[16,2048]{1,0:T(8,128)(2,1)S(1)}, f32[16,2048]{1,0:T(8,128)}) fusion(f32[2048]{0:T(1024)S(1)} %copy-done, f32[16,2048]{1,0:T(8,128)S(1)} %bitcast_subtract_fusion, bf16[2048,2304]{1,0:T(8,128)(2,1)S(1)} %bitcast.26, bf16[16,128]{1,0:T(8,128)(2,1)S(1)} %collective-permute-done.9, bf16[16,2048]{1,0:T(8,128)(2,1)S(1)} %fusion.6, ...), kind=kOutput, calls=%fused_computation.61 | convolution fusion | flops 151314432 | bytes 9846784 | tf_op jit(solution)/shard_map/dot_general | solution.py:47
  97.6 10.9 %all_to_all.5 = bf16[4,16,2048]{2,1,0:T(8,128)(2,1)S(1)} all-to-all(bf16[4,16,2048]{2,1,0:T(8,128)(2,1)S(1)} %stack.2), channel_id=1, replica_groups=mesh['patch'=32,'grp'=4] {'grp'}, dimensions={0} | all-to-all | bytes 524288 | tf_op jit(solution)/shard_map/all_to_all | solution.py:53
  108.6 0.7 copy.19
  (21 shorter events, 0.1 us)
Async XLA Ops:
  0.6 29.5 %collective-permute-start.1 = (bf16[8,16,8192]{2,1,0:T(8,128)(2,1)}, bf16[8,16,8192]{2,1,0:T(8,128)(2,1)S(1)}, u32[]{:S(2)}, u32[]{:S(2)}) collective-permute-start(bf16[8,16,8192]{2,1,0:T(8,128)(2,1)} %param.12), channel_id=1, source_target_pairs={{4,0},{8,4},{12,8},{16,12},{20,16},{24,20},{28,24},{32,28},{36,32}... | collective-permute-start | bytes 6291464 | tf_op jit(solution)/shard_map/ppermute | solution.py:21
  6.3 29.8 %collective-permute-start = (bf16[8,16,8192]{2,1,0:T(8,128)(2,1)}, bf16[8,16,8192]{2,1,0:T(8,128)(2,1)}, u32[]{:S(2)}, u32[]{:S(2)}) collective-permute-start(bf16[8,16,8192]{2,1,0:T(8,128)(2,1)} %param.12), channel_id=1, source_target_pairs={{0,4},{4,8},{8,12},{12,16},{16,20},{20,24},{24,28},{28,32},{32,36}... | collective-permute-start | bytes 6291464 | tf_op jit(solution)/shard_map/ppermute | solution.py:18
  9.2 46.8 %collective-permute-start.3 = (bf16[16,128]{1,0:T(8,128)(2,1)S(1)}, bf16[16,128]{1,0:T(8,128)(2,1)S(1)}, u32[]{:S(2)}, u32[]{:S(2)}) collective-permute-start(bf16[16,128]{1,0:T(8,128)(2,1)S(1)} %get-tuple-element.9), channel_id=1, source_target_pairs={{4,0},{8,4},{12,8},{16,12},{20,16},{24,20},{28,24},{32,28},{36,32}... | collective-permute-start | bytes 12296 | tf_op jit(solution)/shard_map/ppermute | solution.py:21
  15.0 41.1 %collective-permute-start.2 = (bf16[16,128]{1,0:T(8,128)(2,1)S(1)}, bf16[16,128]{1,0:T(8,128)(2,1)S(1)}, u32[]{:S(2)}, u32[]{:S(2)}) collective-permute-start(bf16[16,128]{1,0:T(8,128)(2,1)S(1)} %get-tuple-element.8), channel_id=1, source_target_pairs={{0,4},{4,8},{8,12},{12,16},{16,20},{20,24},{24,28},{28,32},{32,36}... | collective-permute-start | bytes 12296 | tf_op jit(solution)/shard_map/ppermute | solution.py:18
  47.2 7.0 %copy-start.2 = (s32[256]{0:T(256)S(1)}, s32[256]{0:T(256)}, u32[]{:S(2)}) copy-start(s32[256]{0:T(256)} %param.14) | copy-start | bytes 3076
  47.3 8.7 %copy-start.1 = (f32[16,2048]{1,0:T(8,128)S(1)}, f32[16,2048]{1,0:T(8,128)}, u32[]{:S(2)}) copy-start(f32[16,2048]{1,0:T(8,128)} %param.9) | copy-start | bytes 393220
  47.3 8.8 %copy-start = (f32[2048]{0:T(1024)S(1)}, f32[2048]{0:T(1024)}, u32[]{:S(2)}) copy-start(f32[2048]{0:T(1024)} %param.10) | copy-start | bytes 24580
  47.3 24.1 %slice-start = ((s8[9437184]{0:T(1024)(128)(4,1)}), s8[4194304]{0:T(1024)(128)(4,1)S(1)}, s32[]{:S(2)}) async-start(s8[9437184]{0:T(1024)(128)(4,1)} %bitcast.25), calls=%async_computation.1 | async-start | bytes 8388608
  47.3 24.1 %slice-start.1 = ((s8[9437184]{0:T(1024)(128)(4,1)}), s8[4194304]{0:T(1024)(128)(4,1)S(1)}, s32[]{:S(2)}) async-start(s8[9437184]{0:T(1024)(128)(4,1)} %bitcast.25), calls=%async_computation.2 | async-start | bytes 8388608
  56.0 15.3 %slice-start.2 = ((s8[9437184]{0:T(1024)(128)(4,1)}), s8[1048576]{0:T(1024)(128)(4,1)S(1)}, s32[]{:S(2)}) async-start(s8[9437184]{0:T(1024)(128)(4,1)} %bitcast.25), calls=%async_computation.3 | async-start | bytes 2097152
  62.4 4.3 %collective-permute-start.5 = (bf16[16,128]{1,0:T(8,128)(2,1)S(1)}, bf16[16,128]{1,0:T(8,128)(2,1)S(1)}, u32[]{:S(2)}, u32[]{:S(2)}) collective-permute-start(bf16[16,128]{1,0:T(8,128)(2,1)S(1)} %get-tuple-element.7), channel_id=1, source_target_pairs={{4,0},{8,4},{12,8},{16,12},{20,16},{24,20},{28,24},{32,28},{36,32}... | collective-permute-start | bytes 12296 | tf_op jit(solution)/shard_map/ppermute | solution.py:21
  64.3 7.0 %collective-permute-start.4 = (bf16[16,128]{1,0:T(8,128)(2,1)S(1)}, bf16[16,128]{1,0:T(8,128)(2,1)S(1)}, u32[]{:S(2)}, u32[]{:S(2)}) collective-permute-start(bf16[16,128]{1,0:T(8,128)(2,1)S(1)} %get-tuple-element.6), channel_id=1, source_target_pairs={{0,4},{4,8},{8,12},{12,16},{16,20},{20,24},{24,28},{28,32},{32,36}... | collective-permute-start | bytes 12296 | tf_op jit(solution)/shard_map/ppermute | solution.py:18
  73.9 4.3 %collective-permute-start.7 = (bf16[16,128]{1,0:T(8,128)(2,1)S(1)}, bf16[16,128]{1,0:T(8,128)(2,1)S(1)}, u32[]{:S(2)}, u32[]{:S(2)}) collective-permute-start(bf16[16,128]{1,0:T(8,128)(2,1)S(1)} %get-tuple-element.5), channel_id=1, source_target_pairs={{4,0},{8,4},{12,8},{16,12},{20,16},{24,20},{28,24},{32,28},{36,32}... | collective-permute-start | bytes 12296 | tf_op jit(solution)/shard_map/ppermute | solution.py:21
  75.9 7.0 %collective-permute-start.6 = (bf16[16,128]{1,0:T(8,128)(2,1)S(1)}, bf16[16,128]{1,0:T(8,128)(2,1)S(1)}, u32[]{:S(2)}, u32[]{:S(2)}) collective-permute-start(bf16[16,128]{1,0:T(8,128)(2,1)S(1)} %get-tuple-element.4), channel_id=1, source_target_pairs={{0,4},{4,8},{8,12},{12,16},{16,20},{20,24},{24,28},{28,32},{32,36}... | collective-permute-start | bytes 12296 | tf_op jit(solution)/shard_map/ppermute | solution.py:18
  85.5 4.3 %collective-permute-start.9 = (bf16[16,128]{1,0:T(8,128)(2,1)S(1)}, bf16[16,128]{1,0:T(8,128)(2,1)S(1)}, u32[]{:S(2)}, u32[]{:S(2)}) collective-permute-start(bf16[16,128]{1,0:T(8,128)(2,1)S(1)} %get-tuple-element.3), channel_id=1, source_target_pairs={{4,0},{8,4},{12,8},{16,12},{20,16},{24,20},{28,24},{32,28},{36,32}... | collective-permute-start | bytes 12296 | tf_op jit(solution)/shard_map/ppermute | solution.py:21
  87.4 7.0 %collective-permute-start.8 = (bf16[16,128]{1,0:T(8,128)(2,1)S(1)}, bf16[16,128]{1,0:T(8,128)(2,1)S(1)}, u32[]{:S(2)}, u32[]{:S(2)}) collective-permute-start(bf16[16,128]{1,0:T(8,128)(2,1)S(1)} %get-tuple-element.2), channel_id=1, source_target_pairs={{0,4},{4,8},{8,12},{12,16},{16,20},{20,24},{24,28},{28,32},{32,36}... | collective-permute-start | bytes 12296 | tf_op jit(solution)/shard_map/ppermute | solution.py:18
